TPU v7x, 256 devices: a whole 4x4x8 slice. The times are simulated.
256 devices in a mesh: lat: 8 (over x, y_lo), lon: 32 (over z, y_hi, core).
Axes of the slice: x: 4, y: 4 (y_hi: 2, y_lo: 2; y = y_hi * 2 + y_lo), z: 8, core: 2. Of those that a mesh axis runs over, the one named last changes fastest.
Arguments:
- inputs: bfloat16 [128, 4096, 64], P('lat', 'lon'), may hold values from -6 to 6
- pre_first: bfloat16 [128, 4096, 128], P('lat', 'lon'), may hold values from -6 to 6
- grad_out: bfloat16 [64, 2048, 128], P('lat', 'lon'), may hold values from -6 to 6
- w_first: bfloat16 [3, 3, 64, 128], replicated, may hold values from -0.25 to 0.25
- w_second: bfloat16 [3, 3, 128, 128], replicated, may hold values from -0.1875 to 0.1875
Outputs:
- grad_inputs: bfloat16 [128, 4096, 64], P('lat', 'lon')
- grad_w_first: float32 [3, 3, 64, 128], replicated
- grad_w_second: float32 [3, 3, 128, 128], replicated
All inputs are finite; a program needn't handle non-finite values.
Results may differ from a plain program's by a relative error of at most 0.0049.
Values may be sent and summed in bfloat16 or wider, within the bound.
A program may use at most 64 MiB of HBM per device.

v0:
```python
import jax
import jax.numpy as jnp
from jax import lax
from jax.sharding import PartitionSpec as P

inv_root = 0.7071067811865476
density = 0.3989422804014327


def passed_along(shard, axis, by):
    peers = lax.axis_size(axis)
    return lax.ppermute(shard, axis, [(i, (i + by) % peers) for i in range(peers)])


def extended(block, sides, width):
    for axis, dim in sides:
        count = lax.axis_size(axis)
        forward = [(i, i + 1) for i in range(count - 1)]
        forward.append((count - 1, 0))
        backward = [(target, source) for source, target in forward]
        low = lax.ppermute(
            lax.slice_in_dim(block, block.shape[dim] - width, None, axis=dim), axis, forward
        )
        high = lax.ppermute(lax.slice_in_dim(block, 0, width, axis=dim), axis, backward)
        block = jnp.concatenate([low, block, high], axis=dim)
    return block


def across_values(row):
    return passed_along(row, "lon", lax.axis_size("lon") // 2)


def across_grads(row):
    return passed_along(row, "lon", lax.axis_size("lon") // 2)


def pad_values(fields):
    band = lax.axis_index("lat")
    padded = extended(fields, (("lat", 0), ("lon", 1)), 1)
    opposite = across_values(padded[1])
    top = jnp.where(band == 0, opposite, padded[0])
    bottom = jnp.where(band == lax.axis_size("lat") - 1, jnp.zeros_like(padded[-1]), padded[-1])
    return jnp.concatenate([top[None], padded[1:-1], bottom[None]], 0)


def fold_grads(grid):
    band = lax.axis_index("lat")
    first = band == 0
    final = band == lax.axis_size("lat") - 1
    opposite = across_grads(grid[0])
    row_one = grid[1] + jnp.where(first, opposite, jnp.zeros_like(opposite))
    top = jnp.where(first, jnp.zeros_like(grid[0]), grid[0])
    bottom = jnp.where(final, jnp.zeros_like(grid[-1]), grid[-1])
    grid = jnp.concatenate([top[None], row_one[None], grid[2:-1], bottom[None]], 0)
    wide = extended(grid, (("lat", 0), ("lon", 1)), 1)
    inner = wide[2:-2]
    inner = inner.at[0].add(wide[0]).at[-1].add(wide[-1])
    core = inner[:, 2:-2]
    core = core.at[:, 0].add(inner[:, 0]).at[:, -1].add(inner[:, -1])
    return core


def taps_product(padded, grads):
    rows, cols = (grads.shape[0], grads.shape[1])
    flat = grads.reshape(rows * cols, grads.shape[2])
    result = []
    for a in range(3):
        line = []
        for b in range(3):
            piece = padded[a : a + rows, b : b + cols].reshape(rows * cols, padded.shape[2])
            line.append(
                lax.dot_general(
                    piece, flat, (((0,), (0,)), ((), ())), preferred_element_type=jnp.float32
                )
            )
        result.append(jnp.stack(line, 0))
    return jnp.stack(result, 0)


def spread(grads, weight):
    rows, cols, cout = grads.shape
    cin = weight.shape[2]
    every = jnp.transpose(weight, (3, 0, 1, 2)).reshape(cout, 9 * cin)
    terms = jnp.dot(grads.reshape(rows * cols, cout), every, preferred_element_type=jnp.float32)
    terms = terms.reshape(rows, cols, 3, 3, cin)
    grid = jnp.zeros((rows + 2, cols + 2, cin), jnp.float32)
    for a in range(3):
        for b in range(3):
            grid = grid.at[a : a + rows, b : b + cols].add(terms[:, :, a, b])
    return grid


def body(inputs, pre_first, grad_out, w_first, w_second):
    first_ch = inputs.shape[2]
    value = pre_first.astype(jnp.float32)
    cdf = 0.5 * (1.0 + lax.erf(value * inv_root))
    activated = (value * cdf).astype(jnp.bfloat16)
    slope = cdf + value * jnp.exp(-0.5 * value * value) * density
    padded = pad_values(jnp.concatenate([inputs, activated], 2))
    padded_in = padded[:, :, :first_ch]
    padded_act = padded[:, :, first_ch:]
    grad_pool = jnp.repeat(jnp.repeat(grad_out, 2, 0), 2, 1) * jnp.asarray(0.25, grad_out.dtype)
    local_second = taps_product(padded_act, grad_pool)
    grad_act = fold_grads(spread(grad_pool, w_second))
    grad_pre = (grad_act * slope).astype(jnp.bfloat16)
    local_first = taps_product(padded_in, grad_pre)
    grad_inputs = fold_grads(spread(grad_pre, w_first)).astype(jnp.bfloat16)
    grad_w_first, grad_w_second = lax.psum((local_first, local_second), ("lat", "lon"))
    return (grad_inputs, grad_w_first, grad_w_second)


def solution(mesh):
    in_specs = (P("lat", "lon", None), P("lat", "lon", None), P("lat", "lon", None), P(), P())
    out_specs = (P("lat", "lon", None), P(), P())
    return jax.shard_map(body, mesh=mesh, in_specs=in_specs, out_specs=out_specs, check_vma=False)
```

profile of v0, /device:TPU:1, one launch (start us, length us, event | category | flops | bytes accessed | tf_op | source)
XLA Modules:
  0.0 447.3 jit_solution(18419216473036246453)
XLA Ops:
  14.6 3.4 scatter-add.89
  18.0 3.4 add_select_fusion
  21.3 3.5 scatter-add.90
  27.6 2.1 scatter-add.94
  31.1 2.1 scatter-add.95
  36.0 2.1 scatter-add.99
  39.5 2.1 scatter-add.100
  41.6 2.2 collective-permute-start
  43.8 3.9 collective-permute-done
  47.7 7.1 %collective-permute-start.1 = (f32[130,128]{1,0:T(8,128)S(1)}, f32[130,128]{1,0:T(8,128)S(1)}, u32[]{:S(2)}, u32[]{:S(2)}) collective-permute-start(f32[130,128]{1,0:T(8,128)S(1)} %get-tuple-element.325), channel_id=1, source_target_pairs={{0,16},{1,17},{2,18},{3,19},{4,20},{5,21},{6,22},{7,23},{8,24},{9,... | collective-permute-start | bytes 199688 | tf_op jit(solution)/shard_map/ppermute | solution.py:12
  58.3 5.8 %collective-permute-start.3 = (f32[20,1,128]{2,1,0:T(1,128)S(1)}, f32[20,1,128]{2,1,0:T(1,128)S(1)}, u32[]{:S(2)}, u32[]{:S(2)}) collective-permute-start(f32[20,1,128]{2,1,0:T(1,128)S(1)} %get-tuple-element.321), channel_id=1, source_target_pairs={{0,1},{1,2},{2,3},{3,4},{4,5},{5,6},{6,7},{7,8},{8,9},{9,10},{10,1... | collective-permute-start | bytes 30728 | tf_op jit(solution)/shard_map/ppermute | solution.py:21
  65.0 3.8 collective-permute-done.4
  73.5 3.0 fusion.69
  77.6 3.3 fusion.68
  81.3 3.6 collective-permute-start.11
  84.8 6.0 %scatter-add.110 = f32[18,130,64]{1,2,0:T(8,128)S(1)} dynamic-update-slice(f32[18,130,64]{1,2,0:T(8,128)S(1)} %scatter-add.109, f32[16,128,64]{1,2,0:T(8,128)} %fusion.68, s32[]{:T(128)} %bitcast.10, s32[]{:T(128)} %bitcast.11, s32[]{:T(128)} %constant.655.clone.1) | dynamic-update-slice | bytes 1048580 | tf_op jit(solution)/shard_map/scatter-add | solution.py:89
  90.8 4.0 add_select_fusion.1
  94.8 6.0 %scatter-add.111 = f32[18,130,64]{1,2,0:T(8,128)S(1)} dynamic-update-slice(f32[18,130,64]{1,2,0:T(8,128)S(1)} %scatter-add.110, f32[16,128,64]{1,2,0:T(8,128)} %add_select_fusion.1, s32[]{:T(128)} %bitcast.13, s32[]{:T(128)} %bitcast.14, s32[]{:T(128)} %constant.655.clone.1) | dynamic-update-slice | bytes 1048580 | tf_op jit(solution)/shard_map/scatter-add | solution.py:89
  102.1 2.0 fusion.65
  104.1 4.7 %scatter-add.115 = f32[18,130,64]{1,2,0:T(8,128)S(1)} dynamic-update-slice(f32[18,130,64]{1,2,0:T(8,128)S(1)} %fusion.67, f32[16,128,64]{1,2,0:T(8,128)} %fusion.65, s32[]{:T(128)} %constant.660.clone.1, s32[]{:T(128)} %constant.660.clone.1, s32[]{:T(128)} %constant.655.clone.1) | dynamic-update-slice | bytes 1048580 | tf_op jit(solution)/shard_map/scatter-add | solution.py:89
  108.8 2.0 fusion.64
  110.8 4.7 %scatter-add.116 = f32[18,130,64]{1,2,0:T(8,128)S(1)} dynamic-update-slice(f32[18,130,64]{1,2,0:T(8,128)S(1)} %scatter-add.115, f32[16,128,64]{1,2,0:T(8,128)} %fusion.64, s32[]{:T(128)} %constant.660.clone.1, s32[]{:T(128)} %constant.656.clone.1, s32[]{:T(128)} %constant.655.clone.1) | dynamic-update-slice | bytes 1048580 | tf_op jit(solution)/shard_map/scatter-add | solution.py:89
  116.7 2.0 fusion.61
  118.7 4.7 %scatter-add.120 = f32[18,130,64]{1,2,0:T(8,128)S(1)} dynamic-update-slice(f32[18,130,64]{1,2,0:T(8,128)S(1)} %fusion.63, f32[16,128,64]{1,2,0:T(8,128)} %fusion.61, s32[]{:T(128)} %constant.656.clone.1, s32[]{:T(128)} %constant.660.clone.1, s32[]{:T(128)} %constant.655.clone.1) | dynamic-update-slice | bytes 1048580 | tf_op jit(solution)/shard_map/scatter-add | solution.py:89
  123.4 2.0 fusion.60
  125.4 4.7 %scatter-add.121 = f32[18,130,64]{1,2,0:T(8,128)S(1)} dynamic-update-slice(f32[18,130,64]{1,2,0:T(8,128)S(1)} %scatter-add.120, f32[16,128,64]{1,2,0:T(8,128)} %fusion.60, s32[]{:T(128)} %constant.656.clone.1, s32[]{:T(128)} %constant.656.clone.1, s32[]{:T(128)} %constant.655.clone.1) | dynamic-update-slice | bytes 1048580 | tf_op jit(solution)/shard_map/scatter-add | solution.py:89
  131.6 4.6 %collective-permute-done.5 = f32[1,130,64]{1,2,0:T(8,128)S(1)} collective-permute-done((f32[1,130,64]{1,2,0:T(8,128)S(1)}, f32[1,130,64]{1,2,0:T(8,128)S(1)}, u32[]{:S(2)}, u32[]{:S(2)}) %collective-permute-start.5) | collective-permute-done | bytes 33312 | tf_op jit(solution)/shard_map/ppermute | solution.py:21
  137.4 4.8 %collective-permute-start.6 = (f32[130,64]{0,1:T(8,128)S(1)}, f32[130,64]{0,1:T(8,128)S(1)}, u32[]{:S(2)}, u32[]{:S(2)}) collective-permute-start(f32[130,64]{0,1:T(8,128)S(1)} %get-tuple-element.330), channel_id=1, source_target_pairs={{0,16},{1,17},{2,18},{3,19},{4,20},{5,21},{6,22},{7,23},{8,24},{9,... | collective-permute-start | bytes 99848 | tf_op jit(solution)/shard_map/ppermute | solution.py:12
  151.0 5.4 %collective-permute-start.14 = (bf16[130,192]{1,0:T(8,128)(2,1)}, bf16[130,192]{1,0:T(8,128)(2,1)}, u32[]{:S(2)}, u32[]{:S(2)}) collective-permute-start(bf16[130,192]{1,0:T(8,128)(2,1)} %get-tuple-element.326), channel_id=1, source_target_pairs={{0,16},{1,17},{2,18},{3,19},{4,20},{5,21},{6,22},{7,23},{8,24},{9,... | collective-permute-start | bytes 149768 | tf_op jit(solution)/shard_map/ppermute | solution.py:12
  162.1 2.0 copy.59
  186.1 250.8 %all-reduce.5.cloned.1.call-done = (f32[3,3,64,128]{3,2,1,0:T(8,128)}, f32[3,3,128,128]{3,2,1,0:T(8,128)}) async-done(((f32[3,3,64,128]{3,2,1,0:T(8,128)}, f32[3,3,128,128]{3,2,1,0:T(8,128)}), (f32[3,3,64,128]{3,2,1,0:T(8,128)}, f32[3,3,128,128]{3,2,1,0:T(8,128)})) %all-reduce.5.cloned.1.call-update) | async-done | bytes 884752 | tf_op jit(solution)/shard_map/psum | solution.py:108
  438.6 1.9 copy.152
  (178 shorter events, 68.7 us)
Async XLA Ops:
  7.2 429.7 %all-reduce.5.cloned.1.call-start = ((), (), s32[]{:S(2)}) async-start(), calls=%async_computation | async-start | bytes 1769472 | tf_op jit(solution)/shard_map/psum | solution.py:108
  10.1 3.7 copy-start.1
  12.2 1.7 copy-start.30
  41.6 6.1 %collective-permute-start = (f32[1,130,128]{2,1,0:T(8,128)S(1)}, f32[1,130,128]{2,1,0:T(8,128)S(1)}, u32[]{:S(2)}, u32[]{:S(2)}) collective-permute-start(f32[1,130,128]{2,1,0:T(8,128)S(1)} %slice_select_fusion), channel_id=1, source_target_pairs={{0,32},{32,64},{64,96},{96,128},{128,160},{160,192},{192,224},{224... | collective-permute-start | bytes 199688 | tf_op jit(solution)/shard_map/ppermute | solution.py:21
  47.7 8.9 %collective-permute-start.1 = (f32[130,128]{1,0:T(8,128)S(1)}, f32[130,128]{1,0:T(8,128)S(1)}, u32[]{:S(2)}, u32[]{:S(2)}) collective-permute-start(f32[130,128]{1,0:T(8,128)S(1)} %get-tuple-element.325), channel_id=1, source_target_pairs={{0,16},{1,17},{2,18},{3,19},{4,20},{5,21},{6,22},{7,23},{8,24},{9,... | collective-permute-start | bytes 199688 | tf_op jit(solution)/shard_map/ppermute | solution.py:12
  54.8 3.5 collective-permute-start.2
  56.6 7.5 %copy-start.18 = (bf16[16,128,64]{1,2,0:T(8,128)(2,1)S(1)}, bf16[16,128,64]{1,2,0:T(8,128)(2,1)}, u32[]{:S(2)}) copy-start(bf16[16,128,64]{1,2,0:T(8,128)(2,1)} %param.57) | copy-start | bytes 786436
  58.3 6.6 %collective-permute-start.3 = (f32[20,1,128]{2,1,0:T(1,128)S(1)}, f32[20,1,128]{2,1,0:T(1,128)S(1)}, u32[]{:S(2)}, u32[]{:S(2)}) collective-permute-start(f32[20,1,128]{2,1,0:T(1,128)S(1)} %get-tuple-element.321), channel_id=1, source_target_pairs={{0,1},{1,2},{2,3},{3,4},{4,5},{5,6},{6,7},{7,8},{8,9},{9,10},{10,1... | collective-permute-start | bytes 30728 | tf_op jit(solution)/shard_map/ppermute | solution.py:21
  64.1 4.6 %collective-permute-start.4 = (f32[20,1,128]{2,1,0:T(1,128)S(1)}, f32[20,1,128]{2,1,0:T(1,128)S(1)}, u32[]{:S(2)}, u32[]{:S(2)}) collective-permute-start(f32[20,1,128]{2,1,0:T(1,128)S(1)} %get-tuple-element.322), channel_id=1, source_target_pairs={{1,0},{2,1},{3,2},{4,3},{5,4},{6,5},{7,6},{8,7},{9,8},{10,9},{11,1... | collective-permute-start | bytes 30728 | tf_op jit(solution)/shard_map/ppermute | solution.py:24
  64.4 77.8 %copy-start.7 = (bf16[16,128,64]{2,1,0:T(8,128)(2,1)}, bf16[16,128,64]{2,1,0:T(8,128)(2,1)S(1)}, u32[]{:S(2)}) copy-start(bf16[16,128,64]{2,1,0:T(8,128)(2,1)S(1)} %copy.62) | copy-start | bytes 786436
  71.0 2.5 copy-start.24
  72.7 69.5 %copy-start.2 = (bf16[16,128,128]{2,1,0:T(8,128)(2,1)}, bf16[16,128,128]{2,1,0:T(8,128)(2,1)S(1)}, u32[]{:S(2)}) copy-start(bf16[16,128,128]{2,1,0:T(8,128)(2,1)S(1)} %get-tuple-element.333) | copy-start | bytes 1572868
  81.2 55.0 %collective-permute-start.10 = (bf16[1,128,192]{2,1,0:T(8,128)(2,1)S(1)}, bf16[1,128,192]{2,1,0:T(8,128)(2,1)S(1)}, u32[]{:S(2)}, u32[]{:S(2)}) collective-permute-start(bf16[1,128,192]{2,1,0:T(8,128)(2,1)S(1)} %get-tuple-element.331), channel_id=1, source_target_pairs={{0,32},{32,64},{64,96},{96,128},{128,160},{160,192},{192,224},{224... | collective-permute-start | bytes 147464 | tf_op jit(solution)/shard_map/ppermute | solution.py:21
  81.3 54.9 %collective-permute-start.11 = (bf16[1,128,192]{2,1,0:T(8,128)(2,1)S(1)}, bf16[1,128,192]{2,1,0:T(8,128)(2,1)S(1)}, u32[]{:S(2)}, u32[]{:S(2)}) collective-permute-start(bf16[1,128,192]{2,1,0:T(8,128)(2,1)S(1)} %get-tuple-element.332), channel_id=1, source_target_pairs={{32,0},{64,32},{96,64},{128,96},{160,128},{192,160},{224,192},{0,2... | collective-permute-start | bytes 147464 | tf_op jit(solution)/shard_map/ppermute | solution.py:24
  130.1 6.0 %collective-permute-start.5 = (f32[1,130,64]{1,2,0:T(8,128)S(1)}, f32[1,130,64]{1,2,0:T(8,128)S(1)}, u32[]{:S(2)}, u32[]{:S(2)}) collective-permute-start(f32[1,130,64]{1,2,0:T(8,128)S(1)} %slice_select_fusion.1), channel_id=1, source_target_pairs={{0,32},{32,64},{64,96},{96,128},{128,160},{160,192},{192,224},{224... | collective-permute-start | bytes 99848 | tf_op jit(solution)/shard_map/ppermute | solution.py:21
  136.3 5.9 %collective-permute-start.12 = (bf16[18,1,192]{2,1,0:T(2,128)(2,1)S(1)}, bf16[18,1,192]{2,1,0:T(2,128)(2,1)S(1)}, u32[]{:S(2)}, u32[]{:S(2)}) collective-permute-start(bf16[18,1,192]{2,1,0:T(2,128)(2,1)S(1)} %get-tuple-element.328), channel_id=1, source_target_pairs={{0,1},{1,2},{2,3},{3,4},{4,5},{5,6},{6,7},{7,8},{8,9},{9,10},{10,1... | collective-permute-start | bytes 20744 | tf_op jit(solution)/shard_map/ppermute | solution.py:21
  137.4 4.8 %collective-permute-start.13 = (bf16[18,1,192]{2,1,0:T(2,128)(2,1)S(1)}, bf16[18,1,192]{2,1,0:T(2,128)(2,1)S(1)}, u32[]{:S(2)}, u32[]{:S(2)}) collective-permute-start(bf16[18,1,192]{2,1,0:T(2,128)(2,1)S(1)} %get-tuple-element.329), channel_id=1, source_target_pairs={{1,0},{2,1},{3,2},{4,3},{5,4},{6,5},{7,6},{8,7},{9,8},{10,9},{11,1... | collective-permute-start | bytes 20744 | tf_op jit(solution)/shard_map/ppermute | solution.py:24
  137.4 22.9 %collective-permute-start.6 = (f32[130,64]{0,1:T(8,128)S(1)}, f32[130,64]{0,1:T(8,128)S(1)}, u32[]{:S(2)}, u32[]{:S(2)}) collective-permute-start(f32[130,64]{0,1:T(8,128)S(1)} %get-tuple-element.330), channel_id=1, source_target_pairs={{0,16},{1,17},{2,18},{3,19},{4,20},{5,21},{6,22},{7,23},{8,24},{9,... | collective-permute-start | bytes 99848 | tf_op jit(solution)/shard_map/ppermute | solution.py:12
  142.2 18.2 %collective-permute-start.7 = (f32[1,130,64]{1,2,0:T(8,128)S(1)}, f32[1,130,64]{1,2,0:T(8,128)S(1)}, u32[]{:S(2)}, u32[]{:S(2)}) collective-permute-start(f32[1,130,64]{1,2,0:T(8,128)S(1)} %get-tuple-element.318), channel_id=1, source_target_pairs={{32,0},{64,32},{96,64},{128,96},{160,128},{192,160},{224,192},{0,2... | collective-permute-start | bytes 99848 | tf_op jit(solution)/shard_map/ppermute | solution.py:24
  142.2 15.5 %copy-start.20 = (bf16[18,1,192]{2,1,0:T(2,128)(2,1)}, bf16[18,1,192]{2,1,0:T(2,128)(2,1)S(1)}, u32[]{:S(2)}) copy-start(bf16[18,1,192]{2,1,0:T(2,128)(2,1)S(1)} %collective-permute-done.12) | copy-start | bytes 20740
  142.2 16.4 %copy-start.22 = (bf16[18,1,192]{2,1,0:T(2,128)(2,1)}, bf16[18,1,192]{2,1,0:T(2,128)(2,1)S(1)}, u32[]{:S(2)}) copy-start(bf16[18,1,192]{2,1,0:T(2,128)(2,1)S(1)} %collective-permute-done.13) | copy-start | bytes 20740
  143.1 1.9 copy-start.11
  151.0 23.8 %collective-permute-start.14 = (bf16[130,192]{1,0:T(8,128)(2,1)}, bf16[130,192]{1,0:T(8,128)(2,1)}, u32[]{:S(2)}, u32[]{:S(2)}) collective-permute-start(bf16[130,192]{1,0:T(8,128)(2,1)} %get-tuple-element.326), channel_id=1, source_target_pairs={{0,16},{1,17},{2,18},{3,19},{4,20},{5,21},{6,22},{7,23},{8,24},{9,... | collective-permute-start | bytes 149768 | tf_op jit(solution)/shard_map/ppermute | solution.py:12
  162.0 9.2 %copy-start.6 = (f32[20,130,64]{1,2,0:T(8,128)S(1)}, f32[20,130,64]{1,2,0:T(8,128)}, u32[]{:S(2)}) copy-start(f32[20,130,64]{1,2,0:T(8,128)} %copy-done.5) | copy-start | bytes 1996804
  162.0 3.8 collective-permute-start.8
  164.1 5.2 %collective-permute-start.9 = (f32[20,1,64]{2,1,0:T(1,128)}, f32[20,1,64]{2,1,0:T(1,128)}, u32[]{:S(2)}, u32[]{:S(2)}) collective-permute-start(f32[20,1,64]{2,1,0:T(1,128)} %copy.59), channel_id=1, source_target_pairs={{1,0},{2,1},{3,2},{4,3},{5,4},{6,5},{7,6},{8,7},{9,8},{10,9},{11,1... | collective-permute-start | bytes 15368 | tf_op jit(solution)/shard_map/ppermute | solution.py:24
  174.4 1.6 copy-start.9
  174.5 1.6 copy-start.21
  174.5 1.6 copy-start.23
  174.6 3.0 copy-start.15
  174.6 2.4 copy-start.12
  180.5 1.7 copy-start.16
  (15 other events, 16.6 us)
Sparse Core Ops, SparseCore 0:
  182.3 254.5 all-reduce.4
where the time goes:
time: 449 us; the launch traced here: 447 us
  waiting for transfers between devices  267 us (59%)
  local copies, waits for them, and re-layouts  69.3 us (15%)
  other arithmetic  44.8 us (10%)
  starting transfers between devices  32.6 us (7%)
  matrix products  18.6 us (4%)
  between operations  14.9 us (3%)
    psum x1, waiting for transfers between devices, body(): lax.psum((local_first, local_second), ('lat', 'lon'))  251 us
    scatter-add x14, local copies, waits for them, and re-layouts, spread(): grid = grid.at[a:a + rows, b:b + cols].add(terms[:, :, a, b])  46.2 us
    add x10, other arithmetic, spread(): grid = grid.at[a:a + rows, b:b + cols].add(terms[:, :, a, b])  18.6 us
    ppermute x3, starting transfers between devices, passed_along(): lax.ppermute(shard, axis, [(i, (i + by) % peers) for i in range(peers)])  17.3 us
    dot_general x18, matrix products, taps_product(): lax.dot_general(piece, flat, (((0,), (0,)), ((), ())), preferred_element_...  14.2 us
    ppermute x6, starting transfers between devices, extended(): lax.ppermute(lax.slice_in_dim(block, block.shape[dim] - width, None, axis...  9.36 us
    unnamed x69, local copies, waits for them, and re-layouts  9.2 us
  transfers between devices with their start and end apart: 16, of which 8 were waited for; matrix products, arithmetic and copies ran while one was open for 16% of the time, Pallas kernels for 0%

commit v1 on v0

--- a/solution.py
+++ b/solution.py
@@ -1,3 +1,4 @@
+import functools
 import jax
 import jax.numpy as jnp
 from jax import lax
@@ -5,6 +6,15 @@
 
 inv_root = 0.7071067811865476
 density = 0.3989422804014327
+
+
+def work_the_trails(my_tile, row_axis, link_axis):
+    for j in (row_axis, link_axis):
+        my_tile = jax.lax.psum(my_tile, axis_name=j)
+    return my_tile
+
+
+edges_direct = functools.partial(work_the_trails, row_axis="lat", link_axis="lon")
 
 
 def passed_along(shard, axis, by):
@@ -105,7 +115,7 @@
     grad_pre = (grad_act * slope).astype(jnp.bfloat16)
     local_first = taps_product(padded_in, grad_pre)
     grad_inputs = fold_grads(spread(grad_pre, w_first)).astype(jnp.bfloat16)
-    grad_w_first, grad_w_second = lax.psum((local_first, local_second), ("lat", "lon"))
+    grad_w_first, grad_w_second = edges_direct((local_first, local_second))
     return (grad_inputs, grad_w_first, grad_w_second)
 
 

time: 449 us -> 516 us (1.15)
  waiting for transfers between devices: 267 us -> 347 us
  matrix products: 18.6 us -> 10.4 us
    psum x1 -> x2, waiting for transfers between devices: 251 us -> 329 us  [work_the_trails(): my_tile = jax.lax.psum(my_tile, axis_name=j)]
    ppermute x6, starting transfers between devices: 9.36 us -> 15.9 us  [extended(): lax.ppermute(lax.slice_in_dim(block, block.shape[dim] - width, None, axis...]
    dot_general x18, matrix products: 14.2 us -> 8.21 us  [taps_product(): lax.dot_general(piece, flat, (((0,), (0,)), ((), ())), preferred_element_...]
  transfers between devices with their start and end apart: 16 -> 17, of which waited for: 8 -> 10; matrix products, arithmetic and copies ran while one was open for 16% -> 13% of each run, Pallas kernels for 0% -> 0%
where the time goes in v1:
time: 516 us; the launch traced here: 515 us
  waiting for transfers between devices  347 us (67%)
  local copies, waits for them, and re-layouts  64.6 us (13%)
  other arithmetic  41.2 us (8%)
  starting transfers between devices  36.6 us (7%)
  between operations  14.8 us (3%)
  matrix products  10.4 us (2%)
    psum x2, waiting for transfers between devices, work_the_trails(): my_tile = jax.lax.psum(my_tile, axis_name=j)  329 us
    scatter-add x14, local copies, waits for them, and re-layouts, spread(): grid = grid.at[a:a + rows, b:b + cols].add(terms[:, :, a, b])  45.7 us
    add x10, other arithmetic, spread(): grid = grid.at[a:a + rows, b:b + cols].add(terms[:, :, a, b])  17.5 us
    ppermute x6, starting transfers between devices, extended(): lax.ppermute(lax.slice_in_dim(block, block.shape[dim] - width, None, axis...  15.9 us
    ppermute x3, starting transfers between devices, passed_along(): lax.ppermute(shard, axis, [(i, (i + by) % peers) for i in range(peers)])  13.6 us
  transfers between devices with their start and end apart: 17, of which 10 were waited for; matrix products, arithmetic and copies ran while one was open for 13% of the time, Pallas kernels for 0%

profile of v1, /device:TPU:1, one launch (start us, length us, event | category | flops | bytes accessed | tf_op | source)
XLA Modules:
  0.0 514.8 jit_solution(5425706115646145299)
XLA Ops:
  14.4 3.4 scatter-add.89
  17.8 3.1 add_select_fusion
  20.9 3.3 scatter-add.90
  27.0 2.1 scatter-add.94
  30.5 2.1 scatter-add.95
  35.4 2.1 scatter-add.99
  38.9 2.1 scatter-add.100
  41.1 2.2 collective-permute-start
  43.3 3.9 collective-permute-done
  47.2 7.1 %collective-permute-start.1 = (f32[130,128]{1,0:T(8,128)S(1)}, f32[130,128]{1,0:T(8,128)S(1)}, u32[]{:S(2)}, u32[]{:S(2)}) collective-permute-start(f32[130,128]{1,0:T(8,128)S(1)} %get-tuple-element.327), channel_id=1, source_target_pairs={{0,16},{1,17},{2,18},{3,19},{4,20},{5,21},{6,22},{7,23},{8,24},{9,... | collective-permute-start | bytes 199688 | tf_op jit(solution)/shard_map/ppermute | solution.py:22
  57.7 5.8 %collective-permute-start.3 = (f32[20,1,128]{2,1,0:T(1,128)S(1)}, f32[20,1,128]{2,1,0:T(1,128)S(1)}, u32[]{:S(2)}, u32[]{:S(2)}) collective-permute-start(f32[20,1,128]{2,1,0:T(1,128)S(1)} %get-tuple-element.323), channel_id=1, source_target_pairs={{0,1},{1,2},{2,3},{3,4},{4,5},{5,6},{6,7},{7,8},{8,9},{9,10},{10,1... | collective-permute-start | bytes 30728 | tf_op jit(solution)/shard_map/ppermute | solution.py:31
  64.8 3.4 collective-permute-done.4
  76.2 2.3 fusion.68
  79.9 6.0 %scatter-add.110 = f32[18,130,64]{1,2,0:T(8,128)S(1)} dynamic-update-slice(f32[18,130,64]{1,2,0:T(8,128)S(1)} %scatter-add.109, f32[16,128,64]{1,2,0:T(8,128)} %fusion.68, s32[]{:T(128)} %bitcast.10, s32[]{:T(128)} %bitcast.11, s32[]{:T(128)} %constant.655.clone.1) | dynamic-update-slice | bytes 1048580 | tf_op jit(solution)/shard_map/scatter-add | solution.py:99
  85.9 3.8 add_select_fusion.1
  89.7 5.9 %scatter-add.111 = f32[18,130,64]{1,2,0:T(8,128)S(1)} dynamic-update-slice(f32[18,130,64]{1,2,0:T(8,128)S(1)} %scatter-add.110, f32[16,128,64]{1,2,0:T(8,128)} %add_select_fusion.1, s32[]{:T(128)} %bitcast.13, s32[]{:T(128)} %bitcast.14, s32[]{:T(128)} %constant.655.clone.1) | dynamic-update-slice | bytes 1048580 | tf_op jit(solution)/shard_map/scatter-add | solution.py:99
  98.8 4.7 scatter-add.115
  105.5 4.7 scatter-add.116
  111.3 2.0 fusion.61
  113.4 4.7 scatter-add.120
  118.1 2.1 fusion.60
  120.1 4.7 scatter-add.121
  126.1 2.7 collective-permute-start.11
  128.8 2.3 collective-permute-done.5
  133.7 4.4 collective-permute-start.6
  138.0 2.2 collective-permute-start.7
  145.0 2.2 collective-permute-start.14
  149.9 3.0 collective-permute-done.14
  158.3 5.6 %collective-permute-start.8 = (f32[20,1,64]{2,1,0:T(1,128)S(1)}, f32[20,1,64]{2,1,0:T(1,128)S(1)}, u32[]{:S(2)}, u32[]{:S(2)}) collective-permute-start(f32[20,1,64]{2,1,0:T(1,128)S(1)} %copy.58), channel_id=1, source_target_pairs={{0,1},{1,2},{2,3},{3,4},{4,5},{5,6},{6,7},{7,8},{8,9},{9,10},{10,1... | collective-permute-start | bytes 15368 | tf_op jit(solution)/shard_map/ppermute | solution.py:31
  165.3 3.8 collective-permute-done.9
  169.3 64.7 %all-reduce.9.cloned.1.call-done = (f32[3,3,64,128]{3,2,1,0:T(8,128)}, f32[3,3,128,128]{3,2,1,0:T(8,128)}) async-done(((f32[3,3,64,128]{3,2,1,0:T(8,128)}, f32[3,3,128,128]{3,2,1,0:T(8,128)}), (f32[3,3,64,128]{3,2,1,0:T(8,128)}, f32[3,3,128,128]{3,2,1,0:T(8,128)})) %all-reduce.9.cloned.1.call-update) | async-done | bytes 884752 | tf_op jit(solution)/shard_map/psum | solution.py:13
  240.3 264.1 %all-reduce.7.cloned.1.call-done = (f32[3,3,64,128]{3,2,1,0:T(8,128)}, f32[3,3,128,128]{3,2,1,0:T(8,128)}) async-done(((f32[3,3,64,128]{3,2,1,0:T(8,128)}, f32[3,3,128,128]{3,2,1,0:T(8,128)}), (f32[3,3,64,128]{3,2,1,0:T(8,128)}, f32[3,3,128,128]{3,2,1,0:T(8,128)})) %all-reduce.7.cloned.1.call-update) | async-done | bytes 884752 | tf_op jit(solution)/shard_map/psum | solution.py:13
  (143 shorter events, 63.9 us)
Async XLA Ops:
  7.2 1.5 copy-start
  7.2 226.8 %all-reduce.9.cloned.1.call-start = ((), (), s32[]{:S(2)}) async-start(), calls=%async_computation.1 | async-start | bytes 1769472 | tf_op jit(solution)/shard_map/psum | solution.py:13
  8.7 1.4 copy-start.4
  10.1 3.6 copy-start.1
  12.0 1.7 copy-start.11
  41.1 6.1 %collective-permute-start = (f32[1,130,128]{2,1,0:T(8,128)S(1)}, f32[1,130,128]{2,1,0:T(8,128)S(1)}, u32[]{:S(2)}, u32[]{:S(2)}) collective-permute-start(f32[1,130,128]{2,1,0:T(8,128)S(1)} %slice_select_fusion), channel_id=1, source_target_pairs={{0,32},{32,64},{64,96},{96,128},{128,160},{160,192},{192,224},{224... | collective-permute-start | bytes 199688 | tf_op jit(solution)/shard_map/ppermute | solution.py:31
  47.2 8.9 %collective-permute-start.1 = (f32[130,128]{1,0:T(8,128)S(1)}, f32[130,128]{1,0:T(8,128)S(1)}, u32[]{:S(2)}, u32[]{:S(2)}) collective-permute-start(f32[130,128]{1,0:T(8,128)S(1)} %get-tuple-element.327), channel_id=1, source_target_pairs={{0,16},{1,17},{2,18},{3,19},{4,20},{5,21},{6,22},{7,23},{8,24},{9,... | collective-permute-start | bytes 199688 | tf_op jit(solution)/shard_map/ppermute | solution.py:22
  54.2 3.5 collective-permute-start.2
  57.7 7.1 %collective-permute-start.3 = (f32[20,1,128]{2,1,0:T(1,128)S(1)}, f32[20,1,128]{2,1,0:T(1,128)S(1)}, u32[]{:S(2)}, u32[]{:S(2)}) collective-permute-start(f32[20,1,128]{2,1,0:T(1,128)S(1)} %get-tuple-element.323), channel_id=1, source_target_pairs={{0,1},{1,2},{2,3},{3,4},{4,5},{5,6},{6,7},{7,8},{8,9},{9,10},{10,1... | collective-permute-start | bytes 30728 | tf_op jit(solution)/shard_map/ppermute | solution.py:31
  63.6 4.6 collective-permute-start.4
  73.4 2.0 copy-start.10
  76.2 3.2 copy-start.3
  78.6 1.0 copy-start.5
  79.4 52.3 %collective-permute-start.10 = (bf16[1,128,192]{2,1,0:T(8,128)(2,1)}, bf16[1,128,192]{2,1,0:T(8,128)(2,1)S(1)}, u32[]{:S(2)}, u32[]{:S(2)}) collective-permute-start(bf16[1,128,192]{2,1,0:T(8,128)(2,1)} %get-tuple-element.333), channel_id=1, source_target_pairs={{0,32},{32,64},{64,96},{96,128},{128,160},{160,192},{192,224},{224... | collective-permute-start | bytes 147464 | tf_op jit(solution)/shard_map/ppermute | solution.py:31
  118.0 7.9 %copy-start.9 = (bf16[16,128,64]{1,2,0:T(8,128)(2,1)S(1)}, bf16[16,128,64]{1,2,0:T(8,128)(2,1)}, u32[]{:S(2)}) copy-start(bf16[16,128,64]{1,2,0:T(8,128)(2,1)} %param.57) | copy-start | bytes 786436
  124.8 6.3 %collective-permute-start.5 = (f32[1,130,64]{1,2,0:T(8,128)S(1)}, f32[1,130,64]{1,2,0:T(8,128)S(1)}, u32[]{:S(2)}, u32[]{:S(2)}) collective-permute-start(f32[1,130,64]{1,2,0:T(8,128)S(1)} %slice_select_fusion.1), channel_id=1, source_target_pairs={{0,32},{32,64},{64,96},{96,128},{128,160},{160,192},{192,224},{224... | collective-permute-start | bytes 99848 | tf_op jit(solution)/shard_map/ppermute | solution.py:31
  126.1 5.6 %collective-permute-start.11 = (bf16[1,128,192]{2,1,0:T(8,128)(2,1)S(1)}, bf16[1,128,192]{2,1,0:T(8,128)(2,1)S(1)}, u32[]{:S(2)}, u32[]{:S(2)}) collective-permute-start(bf16[1,128,192]{2,1,0:T(8,128)(2,1)S(1)} %get-tuple-element.334), channel_id=1, source_target_pairs={{32,0},{64,32},{96,64},{128,96},{160,128},{192,160},{224,192},{0,2... | collective-permute-start | bytes 147464 | tf_op jit(solution)/shard_map/ppermute | solution.py:34
  131.8 8.4 %collective-permute-start.12 = (bf16[18,1,192]{2,1,0:T(2,128)(2,1)S(1)}, bf16[18,1,192]{2,1,0:T(2,128)(2,1)S(1)}, u32[]{:S(2)}, u32[]{:S(2)}) collective-permute-start(bf16[18,1,192]{2,1,0:T(2,128)(2,1)S(1)} %get-tuple-element.330), channel_id=1, source_target_pairs={{0,1},{1,2},{2,3},{3,4},{4,5},{5,6},{6,7},{7,8},{8,9},{9,10},{10,1... | collective-permute-start | bytes 20744 | tf_op jit(solution)/shard_map/ppermute | solution.py:31
  133.0 7.2 %collective-permute-start.13 = (bf16[18,1,192]{2,1,0:T(2,128)(2,1)S(1)}, bf16[18,1,192]{2,1,0:T(2,128)(2,1)S(1)}, u32[]{:S(2)}, u32[]{:S(2)}) collective-permute-start(bf16[18,1,192]{2,1,0:T(2,128)(2,1)S(1)} %get-tuple-element.331), channel_id=1, source_target_pairs={{1,0},{2,1},{3,2},{4,3},{5,4},{6,5},{7,6},{8,7},{9,8},{10,9},{11,1... | collective-permute-start | bytes 20744 | tf_op jit(solution)/shard_map/ppermute | solution.py:34
  133.7 15.6 %collective-permute-start.6 = (f32[130,64]{0,1:T(8,128)S(1)}, f32[130,64]{0,1:T(8,128)S(1)}, u32[]{:S(2)}, u32[]{:S(2)}) collective-permute-start(f32[130,64]{0,1:T(8,128)S(1)} %get-tuple-element.332), channel_id=1, source_target_pairs={{0,16},{1,17},{2,18},{3,19},{4,20},{5,21},{6,22},{7,23},{8,24},{9,... | collective-permute-start | bytes 99848 | tf_op jit(solution)/shard_map/ppermute | solution.py:22
  138.0 19.7 %collective-permute-start.7 = (f32[1,130,64]{1,2,0:T(8,128)}, f32[1,130,64]{1,2,0:T(8,128)S(1)}, u32[]{:S(2)}, u32[]{:S(2)}) collective-permute-start(f32[1,130,64]{1,2,0:T(8,128)} %get-tuple-element.320), channel_id=1, source_target_pairs={{32,0},{64,32},{96,64},{128,96},{160,128},{192,160},{224,192},{0,2... | collective-permute-start | bytes 99848 | tf_op jit(solution)/shard_map/ppermute | solution.py:34
  141.1 1.0 copy-start.6
  145.0 7.9 %collective-permute-start.14 = (bf16[130,192]{1,0:T(8,128)(2,1)S(1)}, bf16[130,192]{1,0:T(8,128)(2,1)S(1)}, u32[]{:S(2)}, u32[]{:S(2)}) collective-permute-start(bf16[130,192]{1,0:T(8,128)(2,1)S(1)} %get-tuple-element.328), channel_id=1, source_target_pairs={{0,16},{1,17},{2,18},{3,19},{4,20},{5,21},{6,22},{7,23},{8,24},{9,... | collective-permute-start | bytes 149768 | tf_op jit(solution)/shard_map/ppermute | solution.py:22
  155.9 1.7 copy-start.2
  157.6 346.8 %all-reduce.7.cloned.1.call-start = ((), (), s32[]{:S(2)}) async-start(), calls=%async_computation | async-start | bytes 1769472 | tf_op jit(solution)/shard_map/psum | solution.py:13
  158.3 6.7 %collective-permute-start.8 = (f32[20,1,64]{2,1,0:T(1,128)S(1)}, f32[20,1,64]{2,1,0:T(1,128)S(1)}, u32[]{:S(2)}, u32[]{:S(2)}) collective-permute-start(f32[20,1,64]{2,1,0:T(1,128)S(1)} %copy.58), channel_id=1, source_target_pairs={{0,1},{1,2},{2,3},{3,4},{4,5},{5,6},{6,7},{7,8},{8,9},{9,10},{10,1... | collective-permute-start | bytes 15368 | tf_op jit(solution)/shard_map/ppermute | solution.py:31
  164.1 4.9 collective-permute-start.9
  234.9 1.0 copy-start.7
  236.1 1.2 copy-start.8
Sparse Core Ops, SparseCore 0:
  157.7 76.2 all-reduce.8
  236.9 267.4 all-reduce.6
